TPU v7x, 128 devices: a whole 4x4x4 slice. The times are simulated.
128 devices in a mesh: freq: 4 (over x), bl: 32 (over z, y, core).
Axes of the slice: x: 4, y: 4, z: 4, core: 2. Of those that a mesh axis runs over, the one named last changes fastest.
Arguments:
- visibilities: float32 [2, 2, 256, 16384], P(None, None, 'freq', 'bl'), may hold values from -6 to 6
- model: bfloat16 [2, 16, 2, 256, 16384], P(None, None, None, 'freq', 'bl'), may hold values from -1.5 to 1.5
- pairs: int32 [2, 16384, 2], P(None, 'bl'), may hold values from 0 to 511, as said below
- uv: float32 [2, 2, 16384], P(None, None, 'bl'), may hold values from -8 to 8
- held_gains: float32 [32, 2, 2, 16, 512], P('bl'), may hold values from -0.5 to 1.5
- solver_owner: int32 [2], replicated, may hold values from 0 to 31
- facet_owner: int32 [2, 4, 4096, 1], P(None, 'freq', 'bl'), may hold values from 0 to 127; in each aligned block of 128 rows (0 to 127, 128 to 255, ..., all dimensions but the last counted through in order) at most 2 rows name the same one
- subgrid_pos: int32 [2, 4, 4096, 2], P(None, 'freq', 'bl'), may hold values from 0 to 32
Outputs:
- solved_gains: float32 [2, 2, 16, 512], replicated
- residual_facets: float32 [4, 32, 2, 64, 64], P('freq', 'bl')
Inputs may be any that keep to these rules, and one draw needn't show every extreme that they name: `pairs`: every station is the first station of some row in each interval. `facet_owner`: in each interval, at most 2 of the 128 subgrids of one device name the same facet owner.
All inputs are finite; a program needn't handle non-finite values.
Results may differ from a plain program's by a relative error of at most 0.0003.
Values sent between devices are 32-bit elements; how exact they have to be, the bound alone decides.
A program may use at most 192 MiB of HBM per device.

v0:
```python
import math

import jax
import jax.numpy as jnp
from jax import lax
from jax.sharding import PartitionSpec as P

SG = 32
FACET = 64
RPS = 4
ITERS = 4
INTERVALS = 2


damping = 0.5
highest = lax.Precision.HIGHEST


def broadcast(shard, axis, root):
    mine = lax.axis_index(axis) == root
    return lax.psum(jnp.where(mine, shard, jnp.zeros_like(shard)), axis)


def predict(model_re, model_im, vis_re, vis_im, first_re, first_im, second_re, second_im):
    zeta_re = model_re * second_re + model_im * second_im
    zeta_im = model_im * second_re - model_re * second_im
    resid_re = vis_re - jnp.sum(first_re * zeta_re - first_im * zeta_im, axis=0)
    resid_im = vis_im - jnp.sum(first_re * zeta_im + first_im * zeta_re, axis=0)
    return (resid_re, resid_im, zeta_re, zeta_im)


def normal_terms(
    model_re,
    model_im,
    resid_re,
    resid_im,
    zeta_re,
    zeta_im,
    first_re,
    first_im,
    second_re,
    second_im,
    model_power,
):
    left_re = jnp.sum(resid_re * zeta_re + resid_im * zeta_im, axis=1)
    left_im = jnp.sum(resid_im * zeta_re - resid_re * zeta_im, axis=1)
    chi_re = model_re * first_re - model_im * first_im
    chi_im = -(model_im * first_re + model_re * first_im)
    right_re = jnp.sum(resid_re * chi_re - resid_im * chi_im, axis=1)
    right_im = -jnp.sum(resid_re * chi_im + resid_im * chi_re, axis=1)
    left_den = model_power * (second_re[:, 0] ** 2 + second_im[:, 0] ** 2)
    right_den = model_power * (first_re[:, 0] ** 2 + first_im[:, 0] ** 2)
    return (left_re, left_im, right_re, right_im, left_den, right_den)


def phase_image(res_re, res_im, coord_u, coord_v, chan_count):
    pixel_pos = (jnp.arange(SG, dtype=jnp.float32) - SG // 2) / SG
    phase_u = 2.0 * math.pi * pixel_pos[None, :, None] * coord_u[:, None, :]
    phase_v = 2.0 * math.pi * pixel_pos[None, :, None] * coord_v[:, None, :]
    ucos, usin = (jnp.cos(phase_u), jnp.sin(phase_u))
    vcos, vsin = (jnp.cos(phase_v), jnp.sin(phase_v))
    weight_re = res_re[:, None, :] * ucos - res_im[:, None, :] * usin
    weight_im = res_re[:, None, :] * usin + res_im[:, None, :] * ucos
    sub_re = jnp.einsum("jak,jbk->jab", weight_re, vcos, precision=highest) - jnp.einsum(
        "jak,jbk->jab", weight_im, vsin, precision=highest
    )
    sub_im = jnp.einsum("jak,jbk->jab", weight_re, vsin, precision=highest) + jnp.einsum(
        "jak,jbk->jab", weight_im, vcos, precision=highest
    )
    return jnp.stack([sub_re, sub_im], axis=1) / math.sqrt(chan_count * RPS)


def regroup_rows(values, chan_count, count_sub):
    return (
        values.reshape(chan_count, count_sub, RPS)
        .transpose(1, 0, 2)
        .reshape(count_sub, chan_count * RPS)
    )


def subgrid_image(resid_re, resid_im, coords, chan_start, total_channels):
    chan_count = resid_re.shape[0]
    count_sub = resid_re.shape[1] // RPS
    channel = (chan_start + jnp.arange(chan_count, dtype=jnp.int32)).astype(jnp.float32)
    scale_freq = 1.0 + 0.5 * channel / total_channels
    coord_u = regroup_rows(coords[0][None, :] * scale_freq[:, None], chan_count, count_sub)
    coord_v = regroup_rows(coords[1][None, :] * scale_freq[:, None], chan_count, count_sub)
    res_re = regroup_rows(resid_re, chan_count, count_sub)
    res_im = regroup_rows(resid_im, chan_count, count_sub)
    return phase_image(res_re, res_im, coord_u, coord_v, chan_count)


def place_subgrids(received, positions):
    facet_axis = jnp.arange(FACET, dtype=jnp.float32)
    offsets = jnp.arange(SG, dtype=jnp.float32)
    row_hot = (
        facet_axis[None, :, None] == positions[:, 0][:, None, None] + offsets[None, None, :]
    ).astype(jnp.float32)
    col_hot = (
        facet_axis[None, :, None] == positions[:, 1][:, None, None] + offsets[None, None, :]
    ).astype(jnp.float32)
    half_placed = jnp.einsum("jzab,jcb->jzac", received, col_hot, precision=highest)
    return jnp.einsum("jxa,jzac->zxc", row_hot, half_placed, precision=highest)


def body(visibilities, model, pairs, uv, held_gains, solver_owner, facet_owner, subgrid_pos):
    groups = lax.axis_size("freq")
    blocks = lax.axis_size("bl")
    devices = groups * blocks
    chan_count = model.shape[3]
    row_count = model.shape[4]
    stations = held_gains.shape[4]
    count_sub = row_count // RPS
    capacity = max(2, 2 * count_sub // devices)
    total_channels = groups * chan_count
    group_index = lax.axis_index("freq")
    chan_start = group_index * chan_count
    station_axis = jnp.arange(stations, dtype=jnp.int32)
    facets = jnp.zeros((2, FACET, FACET), jnp.float32)
    results = []
    for interval in range(INTERVALS):
        gain_now = broadcast(held_gains[0, interval], "bl", solver_owner[interval])
        first_hot = (pairs[interval, :, 0][:, None] == station_axis[None, :]).astype(jnp.float32)
        second_hot = (pairs[interval, :, 1][:, None] == station_axis[None, :]).astype(jnp.float32)
        model_re = model[interval, :, 0].astype(jnp.float32)
        model_im = model[interval, :, 1].astype(jnp.float32)
        vis_re = visibilities[interval, 0]
        vis_im = visibilities[interval, 1]
        model_power = jnp.sum(model_re * model_re + model_im * model_im, axis=1)

        def station_gains(gain_used):
            first_gain = jnp.einsum("zds,rs->zdr", gain_used, first_hot, precision=highest)
            second_gain = jnp.einsum("zds,rs->zdr", gain_used, second_hot, precision=highest)
            return (
                first_gain[0][:, None, :],
                first_gain[1][:, None, :],
                second_gain[0][:, None, :],
                second_gain[1][:, None, :],
            )

        for sweep_index in range(ITERS):
            first_re, first_im, second_re, second_im = station_gains(gain_now)
            resid_re, resid_im, zeta_re, zeta_im = predict(
                model_re, model_im, vis_re, vis_im, first_re, first_im, second_re, second_im
            )
            left_re, left_im, right_re, right_im, left_den, right_den = normal_terms(
                model_re,
                model_im,
                resid_re,
                resid_im,
                zeta_re,
                zeta_im,
                first_re,
                first_im,
                second_re,
                second_im,
                model_power,
            )

            def to_stations(left_val, right_val):
                return jnp.einsum("dr,rs->ds", left_val, first_hot, precision=highest) + jnp.einsum(
                    "dr,rs->ds", right_val, second_hot, precision=highest
                )

            num_re, num_im, den_all = lax.psum(
                (
                    to_stations(left_re, right_re),
                    to_stations(left_im, right_im),
                    to_stations(left_den, right_den),
                ),
                ("freq", "bl"),
            )
            gain_now = gain_now + damping * jnp.stack([num_re, num_im]) / den_all
        results.append(gain_now)
        first_re, first_im, second_re, second_im = station_gains(gain_now)
        resid_re, resid_im, zeta_re, zeta_im = predict(
            model_re, model_im, vis_re, vis_im, first_re, first_im, second_re, second_im
        )
        owners = facet_owner[interval, 0, :, 0]
        position_src = subgrid_pos[interval, 0].astype(jnp.float32)
        owner_hot = (owners[:, None] == jnp.arange(devices, dtype=jnp.int32)[None, :]).astype(
            jnp.int32
        )
        earlier = jnp.cumsum(owner_hot, axis=0) - owner_hot
        rank_index = jnp.sum(owner_hot * earlier, axis=1)
        slot_index = owners * capacity + rank_index
        slot_hot = (
            slot_index[:, None] == jnp.arange(devices * capacity, dtype=jnp.int32)[None, :]
        ).astype(jnp.float32)
        subgrid_set = subgrid_image(resid_re, resid_im, uv[interval], chan_start, total_channels)
        flat_subs = subgrid_set.reshape(count_sub, 2 * SG * SG)
        outgoing = jnp.einsum("js,jf->sf", slot_hot, flat_subs, precision=highest)
        out_pos = jnp.einsum("js,jt->st", slot_hot, position_src, precision=highest)
        arrived, arrived_pos = (
            lax.all_to_all(outgoing, ("freq", "bl"), split_axis=0, concat_axis=0, tiled=True),
            lax.all_to_all(out_pos, ("freq", "bl"), split_axis=0, concat_axis=0, tiled=True),
        )
        received = arrived.reshape(devices * capacity, 2, SG, SG)
        facets = facets + place_subgrids(received, arrived_pos)
    facets = facets * (2.0 / math.sqrt(INTERVALS * count_sub))
    return (jnp.stack(results), facets[None, None])


def solution(mesh):
    placed = (
        P(None, None, "freq", "bl"),
        P(None, None, None, "freq", "bl"),
        P(None, "bl", None),
        P(None, None, "bl"),
        P("bl", None, None, None, None),
        P(),
        P(None, "freq", "bl", None),
        P(None, "freq", "bl", None),
    )
    return jax.shard_map(
        body,
        mesh=mesh,
        in_specs=placed,
        out_specs=(P(), P("freq", "bl", None, None, None)),
        check_vma=False,
    )
```

profile of v0, /device:TPU:1, one launch (start us, length us, event | category | flops | bytes accessed | tf_op | source)
XLA Modules:
  0.0 1601.3 jit_solution(1857000488765776214)
XLA Ops:
  11.0 11.5 all-to-all-start.1
  28.9 14.8 multiply_cosine_fusion.20
  43.7 14.9 multiply_sine_fusion.30
  58.6 14.7 multiply_cosine_fusion.21
  73.3 14.9 multiply_sine_fusion.31
  88.2 14.8 multiply_cosine_fusion.22
  103.0 14.9 multiply_sine_fusion.28
  117.9 14.9 multiply_cosine_fusion.23
  132.8 14.9 multiply_sine_fusion.29
  151.0 9.8 all-to-all-start.3
  177.6 139.4 %all-reduce.33.cloned.1.call-done = (f32[1,16,512]{2,1,0:T(8,128)}, f32[1,16,512]{2,1,0:T(8,128)}, f32[16,512]{1,0:T(8,128)}) async-done(((f32[1,16,512]{2,1,0:T(8,128)}, f32[1,16,512]{2,1,0:T(8,128)}, f32[16,512]{1,0:T(8,128)}), (f32[1,16,512]{2,1,0:T(8,128)}, f32[1,16,512]{2,1,0:T(8,128)}, f32[16,512]{1,0:T(8,128)})) %all-reduce.33.cloned.1.call-update) | async-done | bytes 98320 | tf_op jit(solution)/shard_map/psum | solution.py:165
  330.1 136.3 %all-reduce.31.cloned.1.call-done = (f32[1,16,512]{2,1,0:T(8,128)}, f32[1,16,512]{2,1,0:T(8,128)}, f32[16,512]{1,0:T(8,128)}) async-done(((f32[1,16,512]{2,1,0:T(8,128)}, f32[1,16,512]{2,1,0:T(8,128)}, f32[16,512]{1,0:T(8,128)}), (f32[1,16,512]{2,1,0:T(8,128)}, f32[1,16,512]{2,1,0:T(8,128)}, f32[16,512]{1,0:T(8,128)})) %all-reduce.31.cloned.1.call-update) | async-done | bytes 98320 | tf_op jit(solution)/shard_map/psum | solution.py:165
  479.7 136.1 %all-reduce.29.cloned.1.call-done = (f32[1,16,512]{2,1,0:T(8,128)}, f32[1,16,512]{2,1,0:T(8,128)}, f32[16,512]{1,0:T(8,128)}) async-done(((f32[1,16,512]{2,1,0:T(8,128)}, f32[1,16,512]{2,1,0:T(8,128)}, f32[16,512]{1,0:T(8,128)}), (f32[1,16,512]{2,1,0:T(8,128)}, f32[1,16,512]{2,1,0:T(8,128)}, f32[16,512]{1,0:T(8,128)})) %all-reduce.29.cloned.1.call-update) | async-done | bytes 98320 | tf_op jit(solution)/shard_map/psum | solution.py:165
  628.2 137.0 %all-reduce.27.cloned.1.call-done = (f32[1,16,512]{2,1,0:T(8,128)}, f32[1,16,512]{2,1,0:T(8,128)}, f32[16,512]{1,0:T(8,128)}) async-done(((f32[1,16,512]{2,1,0:T(8,128)}, f32[1,16,512]{2,1,0:T(8,128)}, f32[16,512]{1,0:T(8,128)}), (f32[1,16,512]{2,1,0:T(8,128)}, f32[1,16,512]{2,1,0:T(8,128)}, f32[16,512]{1,0:T(8,128)})) %all-reduce.27.cloned.1.call-update) | async-done | bytes 98320 | tf_op jit(solution)/shard_map/psum | solution.py:165
  780.1 21.8 %fusion.16 = f32[128,32,32]{2,1,0:T(8,128)S(1)} fusion(f32[128,256]{1,0:T(8,128)S(1)} %copy.74, f32[128,256]{1,0:T(8,128)S(1)} %copy.70, f32[128,256]{1,0:T(8,128)S(1)} %copy.68, f32[32]{0:T(128)S(1)} %add_multiply_fusion, f32[128,32,256]{2,1,0:T(8,128)} %multiply_cosine_fusion.22), kind=kOutput, calls=%fused_computation.100 | convolution fusion | flops 406847488 | bytes 5111936 | tf_op jit(solution)/shard_map/jak,jbk->jab/dot_general | solution.py:67
  801.9 19.4 %add_bitcast_fusion = f32[128,1,32,32]{3,2,0,1:T(8,128)S(1)} fusion(f32[128,32,32]{2,1,0:T(8,128)S(1)} %fusion.16, f32[32]{0:T(128)S(1)} %add_multiply_fusion, f32[128,256]{1,0:T(8,128)S(1)} %copy.74, f32[128,256]{1,0:T(8,128)S(1)} %copy.70, f32[128,256]{1,0:T(8,128)S(1)} %copy.68, f32[128,32,256]{2,1,0:T(8,128)S(1)} %copy-done.10), kind=kOutput, calls=%fused_computation.164 | convolution fusion | flops 406978560 | bytes 5636224 | tf_op jit(solution)/shard_map/jak,jbk->jab/dot_general | solution.py:67
  821.4 22.7 %fusion.17 = f32[128,32,32]{2,1,0:T(8,128)} fusion(f32[128,256]{1,0:T(8,128)S(1)} %copy.74, f32[128,256]{1,0:T(8,128)S(1)} %copy.70, f32[128,256]{1,0:T(8,128)S(1)} %copy.68, f32[32]{0:T(128)S(1)} %add_multiply_fusion, f32[128,32,256]{2,1,0:T(8,128)} %multiply_cosine_fusion.23), kind=kOutput, calls=%fused_computation.101 | convolution fusion | flops 406847488 | bytes 5111936 | tf_op jit(solution)/shard_map/jak,jbk->jab/dot_general | solution.py:64
  844.2 114.3 %all-reduce.25.cloned.1.call-done = (f32[1,16,512]{2,1,0:T(8,128)}, f32[1,16,512]{2,1,0:T(8,128)}, f32[16,512]{1,0:T(8,128)}) async-done(((f32[1,16,512]{2,1,0:T(8,128)}, f32[1,16,512]{2,1,0:T(8,128)}, f32[16,512]{1,0:T(8,128)}), (f32[1,16,512]{2,1,0:T(8,128)}, f32[1,16,512]{2,1,0:T(8,128)}, f32[16,512]{1,0:T(8,128)})) %all-reduce.25.cloned.1.call-update) | async-done | bytes 98320 | tf_op jit(solution)/shard_map/psum | solution.py:165
  970.9 22.7 %subtract_bitcast_fusion = f32[128,1,32,32]{3,2,0,1:T(8,128)} fusion(f32[128,32,32]{2,1,0:T(8,128)} %fusion.17, f32[32]{0:T(128)S(1)} %add_multiply_fusion, f32[128,256]{1,0:T(8,128)S(1)} %copy.74, f32[128,256]{1,0:T(8,128)S(1)} %copy.70, f32[128,256]{1,0:T(8,128)S(1)} %copy.68, f32[128,32,256]{2,1,0:T(8,128)} %multiply_sine_fusion.29), kind=kOutput, calls=%fused_computation.165 | convolution fusion | flops 406978560 | bytes 5636224 | tf_op jit(solution)/shard_map/jak,jbk->jab/dot_general | solution.py:64
  997.6 110.3 %all-reduce.23.cloned.1.call-done = (f32[1,16,512]{2,1,0:T(8,128)}, f32[1,16,512]{2,1,0:T(8,128)}, f32[16,512]{1,0:T(8,128)}) async-done(((f32[1,16,512]{2,1,0:T(8,128)}, f32[1,16,512]{2,1,0:T(8,128)}, f32[16,512]{1,0:T(8,128)}), (f32[1,16,512]{2,1,0:T(8,128)}, f32[1,16,512]{2,1,0:T(8,128)}, f32[16,512]{1,0:T(8,128)})) %all-reduce.23.cloned.1.call-update) | async-done | bytes 98320 | tf_op jit(solution)/shard_map/psum | solution.py:165
  1120.7 136.7 %all-reduce.21.cloned.1.call-done = (f32[1,16,512]{2,1,0:T(8,128)}, f32[1,16,512]{2,1,0:T(8,128)}, f32[16,512]{1,0:T(8,128)}) async-done(((f32[1,16,512]{2,1,0:T(8,128)}, f32[1,16,512]{2,1,0:T(8,128)}, f32[16,512]{1,0:T(8,128)}), (f32[1,16,512]{2,1,0:T(8,128)}, f32[1,16,512]{2,1,0:T(8,128)}, f32[16,512]{1,0:T(8,128)})) %all-reduce.21.cloned.1.call-update) | async-done | bytes 98320 | tf_op jit(solution)/shard_map/psum | solution.py:165
  1279.6 143.0 %all-reduce.19.cloned.1.call-done = (f32[1,16,512]{2,1,0:T(8,128)}, f32[1,16,512]{2,1,0:T(8,128)}, f32[16,512]{1,0:T(8,128)}) async-done(((f32[1,16,512]{2,1,0:T(8,128)}, f32[1,16,512]{2,1,0:T(8,128)}, f32[16,512]{1,0:T(8,128)}), (f32[1,16,512]{2,1,0:T(8,128)}, f32[1,16,512]{2,1,0:T(8,128)}, f32[16,512]{1,0:T(8,128)})) %all-reduce.19.cloned.1.call-update) | async-done | bytes 98320 | tf_op jit(solution)/shard_map/psum | solution.py:165
  1428.6 21.8 %fusion.8 = f32[128,32,32]{2,1,0:T(8,128)S(1)} fusion(f32[128,256]{1,0:T(8,128)S(1)} %copy.55, f32[128,256]{1,0:T(8,128)S(1)} %copy.51, f32[32]{0:T(128)S(1)} %add_multiply_fusion, f32[128,256]{1,0:T(8,128)S(1)} %copy.49, f32[128,32,256]{2,1,0:T(8,128)} %multiply_cosine_fusion.20), kind=kOutput, calls=%fused_computation.92 | convolution fusion | flops 406847488 | bytes 5111936 | tf_op jit(solution)/shard_map/jak,jbk->jab/dot_general | solution.py:67
  1450.4 19.7 %add_bitcast_fusion.1 = f32[128,1,32,32]{3,2,0,1:T(8,128)S(1)} fusion(f32[128,32,32]{2,1,0:T(8,128)S(1)} %fusion.8, f32[32]{0:T(128)S(1)} %add_multiply_fusion, f32[128,256]{1,0:T(8,128)S(1)} %copy.55, f32[128,256]{1,0:T(8,128)S(1)} %copy.51, f32[128,256]{1,0:T(8,128)S(1)} %copy.49, f32[128,32,256]{2,1,0:T(8,128)S(1)} %copy-done.9), kind=kOutput, calls=%fused_computation.186 | convolution fusion | flops 406978560 | bytes 5636224 | tf_op jit(solution)/shard_map/jak,jbk->jab/dot_general | solution.py:67
  1471.4 21.9 %fusion.9 = f32[128,32,32]{2,1,0:T(8,128)S(1)} fusion(f32[128,256]{1,0:T(8,128)S(1)} %copy.55, f32[128,256]{1,0:T(8,128)S(1)} %copy.51, f32[32]{0:T(128)S(1)} %add_multiply_fusion, f32[128,256]{1,0:T(8,128)S(1)} %copy.49, f32[128,32,256]{2,1,0:T(8,128)} %multiply_cosine_fusion.21), kind=kOutput, calls=%fused_computation.93 | convolution fusion | flops 406847488 | bytes 5111936 | tf_op jit(solution)/shard_map/jak,jbk->jab/dot_general | solution.py:64
  1493.3 19.6 %subtract_bitcast_fusion.1 = f32[128,1,32,32]{3,2,0,1:T(8,128)S(1)} fusion(f32[128,32,32]{2,1,0:T(8,128)S(1)} %fusion.9, f32[32]{0:T(128)S(1)} %add_multiply_fusion, f32[128,256]{1,0:T(8,128)S(1)} %copy.55, f32[128,256]{1,0:T(8,128)S(1)} %copy.51, f32[128,256]{1,0:T(8,128)S(1)} %copy.49, f32[128,32,256]{2,1,0:T(8,128)S(1)} %copy-done.8), kind=kOutput, calls=%fused_computation.187 | convolution fusion | flops 406978560 | bytes 5636224 | tf_op jit(solution)/shard_map/jak,jbk->jab/dot_general | solution.py:64
  1525.2 6.9 reshape.450
  1532.1 9.0 fusion.36
  1541.1 13.2 all-to-all-done
  1559.7 7.6 fusion.33
  1567.3 13.3 fusion.140
  1580.6 13.1 fusion.160
  (376 shorter events, 158.1 us)
Async XLA Ops:
  11.0 140.0 %all-to-all-start.1 = ((f32[128,2,2]{2,1,0:T(2,128)}), f32[128,2,2]{2,1,0:T(2,128)S(1)}, u32[]{:S(2)}, u32[]{:S(2)}) async-start(f32[128,2,2]{2,1,0:T(2,128)} %copy.62), calls=%async_computation.1 | async-start | bytes 262144 | tf_op jit(solution)/shard_map/all_to_all | solution.py:196
  22.5 138.4 %all-reduce.35.cloned.1.call-start = ((), (), s32[]{:S(2)}) async-start(), calls=%async_computation.12 | async-start | bytes 262144 | tf_op jit(solution)/shard_map/psum | solution.py:21
  147.7 627.6 %copy-start.69 = (s32[1,512,1]{1,2,0:T(1,128)}, s32[1,512,1]{1,2,0:T(1,128)S(1)}, u32[]{:S(2)}) copy-start(s32[1,512,1]{1,2,0:T(1,128)S(1)} %get-tuple-element.177) | copy-start | bytes 6148
  147.7 631.3 %copy-start.64 = (s32[1,512,1]{1,2,0:T(1,128)}, s32[1,512,1]{1,2,0:T(1,128)S(1)}, u32[]{:S(2)}) copy-start(s32[1,512,1]{1,2,0:T(1,128)S(1)} %get-tuple-element.176) | copy-start | bytes 6148
  151.0 25.1 %all-to-all-start.3 = ((f32[128,2,2]{2,1,0:T(2,128)}), f32[128,2,2]{2,1,0:T(2,128)S(1)}, u32[]{:S(2)}, u32[]{:S(2)}) async-start(f32[128,2,2]{2,1,0:T(2,128)} %copy.81), calls=%async_computation.3 | async-start | bytes 262144 | tf_op jit(solution)/shard_map/all_to_all | solution.py:196
  160.7 156.3 %all-reduce.33.cloned.1.call-start = ((), (), s32[]{:S(2)}) async-start(), calls=%async_computation.11 | async-start | bytes 196608 | tf_op jit(solution)/shard_map/psum | solution.py:165
  170.8 146.3 %copy-start.13 = (f32[2,16,512]{2,1,0:T(8,128)S(1)}, f32[2,16,512]{2,1,0:T(8,128)}, u32[]{:S(2)}) copy-start(f32[2,16,512]{2,1,0:T(8,128)} %get-tuple-element.108) | copy-start | bytes 196612
  175.6 290.8 %all-reduce.31.cloned.1.call-start = ((), (), s32[]{:S(2)}) async-start(), calls=%async_computation.10 | async-start | bytes 196608 | tf_op jit(solution)/shard_map/psum | solution.py:165
  322.5 143.9 %copy-start.16 = (f32[1,16,512]{2,1,0:T(8,128)S(1)}, f32[1,16,512]{2,1,0:T(8,128)}, u32[]{:S(2)}) copy-start(f32[1,16,512]{2,1,0:T(8,128)} %get-tuple-element.105) | copy-start | bytes 98308
  322.5 143.9 %copy-start.17 = (f32[1,16,512]{2,1,0:T(8,128)S(1)}, f32[1,16,512]{2,1,0:T(8,128)}, u32[]{:S(2)}) copy-start(f32[1,16,512]{2,1,0:T(8,128)} %get-tuple-element.106) | copy-start | bytes 98308
  322.5 143.9 %copy-start.18 = (f32[16,512]{1,0:T(8,128)S(1)}, f32[16,512]{1,0:T(8,128)}, u32[]{:S(2)}) copy-start(f32[16,512]{1,0:T(8,128)} %get-tuple-element.107) | copy-start | bytes 98308
  329.4 286.4 %all-reduce.29.cloned.1.call-start = ((), (), s32[]{:S(2)}) async-start(), calls=%async_computation.9 | async-start | bytes 196608 | tf_op jit(solution)/shard_map/psum | solution.py:165
  471.9 143.9 %copy-start.24 = (f32[1,16,512]{2,1,0:T(8,128)S(1)}, f32[1,16,512]{2,1,0:T(8,128)}, u32[]{:S(2)}) copy-start(f32[1,16,512]{2,1,0:T(8,128)} %get-tuple-element.102) | copy-start | bytes 98308
  471.9 143.9 %copy-start.26 = (f32[1,16,512]{2,1,0:T(8,128)S(1)}, f32[1,16,512]{2,1,0:T(8,128)}, u32[]{:S(2)}) copy-start(f32[1,16,512]{2,1,0:T(8,128)} %get-tuple-element.103) | copy-start | bytes 98308
  472.0 143.9 %copy-start.28 = (f32[16,512]{1,0:T(8,128)S(1)}, f32[16,512]{1,0:T(8,128)}, u32[]{:S(2)}) copy-start(f32[16,512]{1,0:T(8,128)} %get-tuple-element.104) | copy-start | bytes 98308
  478.8 286.4 %all-reduce.27.cloned.1.call-start = ((), (), s32[]{:S(2)}) async-start(), calls=%async_computation.8 | async-start | bytes 196608 | tf_op jit(solution)/shard_map/psum | solution.py:165
  621.3 143.9 %copy-start.36 = (f32[1,16,512]{2,1,0:T(8,128)S(1)}, f32[1,16,512]{2,1,0:T(8,128)}, u32[]{:S(2)}) copy-start(f32[1,16,512]{2,1,0:T(8,128)} %get-tuple-element.99) | copy-start | bytes 98308
  621.3 143.9 %copy-start.38 = (f32[1,16,512]{2,1,0:T(8,128)S(1)}, f32[1,16,512]{2,1,0:T(8,128)}, u32[]{:S(2)}) copy-start(f32[1,16,512]{2,1,0:T(8,128)} %get-tuple-element.100) | copy-start | bytes 98308
  621.3 143.9 %copy-start.40 = (f32[16,512]{1,0:T(8,128)S(1)}, f32[16,512]{1,0:T(8,128)}, u32[]{:S(2)}) copy-start(f32[16,512]{1,0:T(8,128)} %get-tuple-element.101) | copy-start | bytes 98308
  628.2 330.3 %all-reduce.25.cloned.1.call-start = ((), (), s32[]{:S(2)}) async-start(), calls=%async_computation.7 | async-start | bytes 196608 | tf_op jit(solution)/shard_map/psum | solution.py:165
  771.8 195.7 %copy-start.54 = (f32[16,512]{1,0:T(8,128)}, f32[16,512]{1,0:T(8,128)S(1)}, u32[]{:S(2)}) copy-start(f32[16,512]{1,0:T(8,128)S(1)} %get-tuple-element.76) | copy-start | bytes 98308
  821.4 286.6 %all-reduce.23.cloned.1.call-start = ((), (), s32[]{:S(2)}) async-start(), calls=%async_computation.6 | async-start | bytes 196608 | tf_op jit(solution)/shard_map/psum | solution.py:165
  970.9 286.5 %all-reduce.21.cloned.1.call-start = ((), (), s32[]{:S(2)}) async-start(), calls=%async_computation.5 | async-start | bytes 196608 | tf_op jit(solution)/shard_map/psum | solution.py:165
  1116.0 142.2 %copy-start.73 = (s32[1,512,1]{1,2,0:T(1,128)S(1)}, s32[1,512,1]{1,2,0:T(1,128)}, u32[]{:S(2)}) copy-start(s32[1,512,1]{1,2,0:T(1,128)} %copy-done.69) | copy-start | bytes 6148
  1116.5 142.4 %copy-start.68 = (s32[1,512,1]{1,2,0:T(1,128)S(1)}, s32[1,512,1]{1,2,0:T(1,128)}, u32[]{:S(2)}) copy-start(s32[1,512,1]{1,2,0:T(1,128)} %copy-done.64) | copy-start | bytes 6148
  1117.0 142.7 %copy-start.56 = (f32[16,512]{1,0:T(8,128)S(1)}, f32[16,512]{1,0:T(8,128)}, u32[]{:S(2)}) copy-start(f32[16,512]{1,0:T(8,128)} %copy-done.54) | copy-start | bytes 98308
  1120.3 302.3 %all-reduce.19.cloned.1.call-start = ((), (), s32[]{:S(2)}) async-start(), calls=%async_computation.4 | async-start | bytes 196608 | tf_op jit(solution)/shard_map/psum | solution.py:165
  1273.7 148.9 %copy-start.42 = (f32[1,16,512]{2,1,0:T(8,128)S(1)}, f32[1,16,512]{2,1,0:T(8,128)}, u32[]{:S(2)}) copy-start(f32[1,16,512]{2,1,0:T(8,128)} %get-tuple-element.87) | copy-start | bytes 98308
  1273.7 148.9 %copy-start.44 = (f32[1,16,512]{2,1,0:T(8,128)S(1)}, f32[1,16,512]{2,1,0:T(8,128)}, u32[]{:S(2)}) copy-start(f32[1,16,512]{2,1,0:T(8,128)} %get-tuple-element.88) | copy-start | bytes 98308
  1273.7 148.9 %copy-start.46 = (f32[16,512]{1,0:T(8,128)S(1)}, f32[16,512]{1,0:T(8,128)}, u32[]{:S(2)}) copy-start(f32[16,512]{1,0:T(8,128)} %get-tuple-element.89) | copy-start | bytes 98308
  1273.7 244.8 %all-to-all-start.2 = ((f32[128,2,2048]{2,1,0:T(2,128)}), f32[128,2,2048]{2,1,0:T(2,128)}, u32[]{:S(2)}, u32[]{:S(2)}) async-start(f32[128,2,2048]{2,1,0:T(2,128)} %copy.80), calls=%async_computation.2 | async-start | bytes 4194304 | tf_op jit(solution)/shard_map/all_to_all | solution.py:195
  1518.5 35.8 %all-to-all-start = ((f32[128,2,2048]{2,1,0:T(2,128)}), f32[128,2,2048]{2,1,0:T(2,128)S(1)}, u32[]{:S(2)}, u32[]{:S(2)}) async-start(f32[128,2,2048]{2,1,0:T(2,128)} %copy.61), calls=%async_computation | async-start | bytes 4194304 | tf_op jit(solution)/shard_map/all_to_all | solution.py:195
  (56 other events, 1853.8 us)
Sparse Core Ops, SparseCore 0:
  27.2 101.4 all-reduce.34
  175.8 141.2 all-reduce.32
  329.5 136.8 all-reduce.30
  478.9 136.8 all-reduce.28
  628.3 136.8 all-reduce.26
  821.5 136.8 all-reduce.24
  971.0 136.9 all-reduce.22
  1120.5 136.8 all-reduce.20
  1269.9 152.7 all-reduce.18
where the time goes:
time: 1610 us; the launch traced here: 1600 us
  waiting for transfers between devices  1070 us (66%)
  matrix products  269 us (17%)
  other arithmetic  177 us (11%)
  local copies, waits for them, and re-layouts  36.8 us (2%)
  starting transfers between devices  33.7 us (2%)
  between operations  17.4 us (1%)
    psum x8, waiting for transfers between devices, body(): lax.psum((to_stations(left_re, right_re), to_stations(left_im, right_im),...  1050 us
    dot_general x2, matrix products, phase_image(): jnp.einsum('jak,jbk->jab', weight_re, vcos, precision=highest)  44.6 us
    dot_general x2, matrix products, phase_image(): jnp.einsum('jak,jbk->jab', weight_im, vcos, precision=highest)  43.6 us
    dot_general x2, matrix products, phase_image(): jnp.einsum('jak,jbk->jab', weight_im, vsin, precision=highest)  42.3 us
    dot_general x2, matrix products, phase_image(): jnp.einsum('jak,jbk->jab', weight_re, vsin, precision=highest)  39.1 us
  transfers between devices with their start and end apart: 13, of which 9 were waited for; matrix products, arithmetic and copies ran while one was open for 19% of the time, Pallas kernels for 0%

commit v1 on v0

v1 whole, which is shorter than its diff:
```python
import functools
import math

import jax
import jax.numpy as jnp
from jax import lax
from jax.experimental import pallas as pl
from jax.experimental.pallas import tpu as pltpu
from jax.sharding import PartitionSpec as P

SG = 32
FACET = 64
RPS = 4
ITERS = 4
INTERVALS = 2
DIRS = 16
STATIONS = 512
ROWS = 512
CH = 64
PLANE = 16
COLUMN = 8
SBLOCKS = STATIONS // 128
MESH = pl.DeviceIdType.MESH
F32 = jnp.float32
BF16 = jnp.bfloat16

damping = 0.5


def split3(x):
    hi = x.astype(BF16)
    rest = x - hi.astype(F32)
    mid = rest.astype(BF16)
    low = (rest - mid.astype(F32)).astype(BF16)
    return hi, mid, low


def solve_kernel(
    model,
    vis,
    prow,
    pcol,
    start,
    gains_out,
    mix_out,
    hot_sr,
    hot_rs,
    power,
    pairgain,
    mix,
    kterm,
    sums,
    arrived,
    partial,
    chunk,
    rs_send,
    rs_recv,
    ex_send,
    ex_recv,
    ag_send,
    ag_recv,
):
    freq = lax.axis_index("freq")
    bl = lax.axis_index("bl")
    core = lax.rem(bl, 2)
    plane = lax.div(bl, 2)
    column = freq * 2 + core

    def plane_peer(step):
        other = lax.rem(plane + step, PLANE)
        return other, (freq, other * 2 + core)

    def column_peer(step):
        other = lax.rem(column + step, COLUMN)
        return other, (lax.div(other, 2), plane * 2 + lax.rem(other, 2))

    barrier = pltpu.get_barrier_semaphore()
    for step in range(1, PLANE):
        pl.semaphore_signal(barrier, inc=1, device_id=plane_peer(step)[1], device_id_type=MESH)
    for step in range(1, COLUMN):
        pl.semaphore_signal(barrier, inc=1, device_id=column_peer(step)[1], device_id_type=MESH)
    pl.semaphore_wait(barrier, PLANE - 1 + COLUMN - 1)

    def exchange(turn, update):
        def rs_copy(step):
            other, device = plane_peer(step)
            return pltpu.make_async_remote_copy(
                src_ref=sums.at[other],
                dst_ref=arrived.at[plane],
                send_sem=rs_send.at[step],
                recv_sem=rs_recv.at[step],
                device_id=device,
                device_id_type=MESH,
            )

        for step in range(1, PLANE):
            rs_copy(step).start()
        arrived[plane] = sums[plane]
        for step in range(1, PLANE):
            rs_copy(step).wait_recv()
        total = arrived[0]
        for m in range(1, PLANE):
            total = total + arrived[m]
        par = lax.rem(turn, 2)
        partial[par, column] = total

        def ex_copy(step):
            _, device = column_peer(step)
            return pltpu.make_async_remote_copy(
                src_ref=partial.at[par, column],
                dst_ref=partial.at[par, column],
                send_sem=ex_send.at[step],
                recv_sem=ex_recv.at[par, step],
                device_id=device,
                device_id_type=MESH,
            )

        for step in range(1, COLUMN):
            ex_copy(step).start()
        for step in range(1, COLUMN):
            ex_copy(step).wait_recv()
        total = partial[par, 0]
        for m in range(1, COLUMN):
            total = total + partial[par, m]
        chunk[plane] = update(total)

        def ag_copy(step):
            _, device = plane_peer(step)
            return pltpu.make_async_remote_copy(
                src_ref=chunk.at[plane],
                dst_ref=chunk.at[plane],
                send_sem=ag_send.at[step],
                recv_sem=ag_recv.at[step],
                device_id=device,
                device_id_type=MESH,
            )

        for step in range(1, PLANE):
            ag_copy(step).start()
        for step in range(1, PLANE):
            rs_copy(step).wait_send()
        for step in range(1, COLUMN):
            ex_copy(step).wait_send()
        for step in range(1, PLANE):
            ag_copy(step).wait_recv()
        for step in range(1, PLANE):
            ag_copy(step).wait_send()

    def pack(interval, table):
        for sb in range(SBLOCKS):
            for dh in range(2):
                for q in range(3):
                    sums[interval * 8 + sb * 2 + dh, q * 8 : q * 8 + 8, :] = table[
                        q * 16 + dh * 8 : q * 16 + dh * 8 + 8, sb * 128 : sb * 128 + 128
                    ]

    for interval in range(INTERVALS):
        pack(interval, start[interval])

    def first_update(total):
        scale = 1.0 / total[16:24]
        return jnp.concatenate([total[0:8] * scale, total[8:16] * scale], axis=0)

    exchange(0, first_update)

    for interval in range(INTERVALS):
        stations = lax.broadcasted_iota(jnp.int32, (STATIONS, 2 * ROWS), 0)
        hot_sr[interval] = (stations == prow[interval]).astype(F32).astype(BF16)
        stations = lax.broadcasted_iota(jnp.int32, (2 * ROWS, STATIONS), 1)
        hot_rs[interval] = (stations == pcol[interval]).astype(F32).astype(BF16)

    def blocks(body):
        def run(index, carry):
            interval = lax.div(index, 4)
            lanes = pl.ds(pl.multiple_of(lax.rem(index, 4) * 128, 128), 128)
            body(interval, lanes)
            return carry

        lax.fori_loop(0, INTERVALS * 4, run, 0)

    def model_at(interval, d, lanes):
        return (
            model[interval, d, 0, :, lanes].astype(F32),
            model[interval, d, 1, :, lanes].astype(F32),
        )

    def power_block(interval, lanes):
        rows = []
        for d in range(DIRS):
            mre, mim = model_at(interval, d, lanes)
            rows.append(jnp.sum(mre * mre + mim * mim, axis=0, keepdims=True))
        power[interval, :, lanes] = jnp.concatenate(rows, axis=0)

    blocks(power_block)

    def gather(interval):
        rows = []
        for z in range(2):
            for dh in range(2):
                rows.append(
                    jnp.concatenate(
                        [
                            chunk[interval * 8 + sb * 2 + dh, z * 8 : z * 8 + 8, :]
                            for sb in range(SBLOCKS)
                        ],
                        axis=1,
                    )
                )
        table = jnp.concatenate(rows, axis=0)
        found = jnp.dot(
            jnp.concatenate(split3(table), axis=0),
            hot_sr[interval],
            preferred_element_type=F32,
        )
        found = found[0:32] + found[32:64] + found[64:96]
        pairgain[interval] = found
        pre, pim = found[0:16, 0:ROWS], found[16:32, 0:ROWS]
        qre, qim = found[0:16, ROWS:], found[16:32, ROWS:]
        mix[interval, 0:16] = pre * qre + pim * qim
        mix[interval, 16:32] = pim * qre - pre * qim
        return table

    def kterm_block(interval, lanes):
        rre, rim = vis[interval, 0, :, lanes], vis[interval, 1, :, lanes]
        for d in range(DIRS):
            mre, mim = model_at(interval, d, lanes)
            wre = mix[interval, d : d + 1, lanes]
            wim = mix[interval, d + 16 : d + 17, lanes]
            rre = rre - (wre * mre - wim * mim)
            rim = rim - (wre * mim + wim * mre)
        real, imag = [], []
        for d in range(DIRS):
            mre, mim = model_at(interval, d, lanes)
            real.append(jnp.sum(rre * mre + rim * mim, axis=0, keepdims=True))
            imag.append(jnp.sum(rim * mre - rre * mim, axis=0, keepdims=True))
        kterm[interval, :, lanes] = jnp.concatenate(real + imag, axis=0)

    def scatter(interval):
        found = pairgain[interval]
        pre, pim = found[0:16, 0:ROWS], found[16:32, 0:ROWS]
        qre, qim = found[0:16, ROWS:], found[16:32, ROWS:]
        kre, kim = kterm[interval, 0:16], kterm[interval, 16:32]
        power_now = power[interval]
        left = jnp.concatenate(
            [qre * kre - qim * kim, qre * kim + qim * kre, power_now * (qre * qre + qim * qim)],
            axis=0,
        )
        right = jnp.concatenate(
            [pre * kre + pim * kim, pim * kre - pre * kim, power_now * (pre * pre + pim * pim)],
            axis=0,
        )
        terms = jnp.concatenate([left, right], axis=1)
        table = jnp.dot(
            jnp.concatenate(split3(terms), axis=0), hot_rs[interval], preferred_element_type=F32
        )
        pack(interval, table[0:48] + table[48:96] + table[96:144])

    def update(total):
        scale = damping / total[16:24]
        return chunk[plane] + jnp.concatenate([total[0:8] * scale, total[8:16] * scale], axis=0)

    def iterate(turn, carry):
        for interval in range(INTERVALS):
            gather(interval)
        blocks(kterm_block)
        for interval in range(INTERVALS):
            scatter(interval)
        exchange(turn, update)
        return carry

    lax.fori_loop(1, ITERS + 1, iterate, 0)
    for interval in range(INTERVALS):
        gains_out[interval] = gather(interval)
        mix_out[interval] = mix[interval]


def solve(model, visibilities, pairs, held, owner):
    bl = lax.axis_index("bl")
    freq = lax.axis_index("freq")
    mine = jnp.logical_and(owner == bl, freq == 0)
    masked = jnp.where(mine[:, None, None, None], held, 0.0).reshape(INTERVALS, 32, STATIONS)
    ones = jnp.broadcast_to(mine.astype(F32)[:, None, None], (INTERVALS, 16, STATIONS))
    start = jnp.concatenate([masked, ones], axis=1)
    prow = pairs.transpose(0, 2, 1).reshape(INTERVALS, 1, 2 * ROWS)
    pcol = prow.reshape(INTERVALS, 2 * ROWS, 1)
    vmem = pl.BlockSpec(memory_space=pltpu.VMEM)
    return pl.pallas_call(
        solve_kernel,
        out_shape=(
            jax.ShapeDtypeStruct((INTERVALS, 32, STATIONS), F32),
            jax.ShapeDtypeStruct((INTERVALS, 32, ROWS), F32),
        ),
        in_specs=[vmem] * 5,
        out_specs=(vmem, vmem),
        scratch_shapes=[
            pltpu.VMEM((INTERVALS, STATIONS, 2 * ROWS), BF16),
            pltpu.VMEM((INTERVALS, 2 * ROWS, STATIONS), BF16),
            pltpu.VMEM((INTERVALS, 16, ROWS), F32),
            pltpu.VMEM((INTERVALS, 32, 2 * ROWS), F32),
            pltpu.VMEM((INTERVALS, 32, ROWS), F32),
            pltpu.VMEM((INTERVALS, 32, ROWS), F32),
            pltpu.VMEM((PLANE, 24, 128), F32),
            pltpu.VMEM((PLANE, 24, 128), F32),
            pltpu.VMEM((2, COLUMN, 24, 128), F32),
            pltpu.VMEM((PLANE, 16, 128), F32),
            pltpu.SemaphoreType.DMA((PLANE,)),
            pltpu.SemaphoreType.DMA((PLANE,)),
            pltpu.SemaphoreType.DMA((COLUMN,)),
            pltpu.SemaphoreType.DMA((2, COLUMN)),
            pltpu.SemaphoreType.DMA((PLANE,)),
            pltpu.SemaphoreType.DMA((PLANE,)),
        ],
        compiler_params=pltpu.CompilerParams(
            collective_id=0, has_side_effects=True, vmem_limit_bytes=48 * 1024 * 1024
        ),
        name="solve",
    )(model, visibilities, prow, pcol, start)


GROUP = 16
HALVES = 2
NSUB = ROWS // RPS


def sincos(x):
    y = x * x
    s = jnp.full_like(x, 1.0 / math.factorial(17))
    c = jnp.full_like(x, 1.0 / math.factorial(16))
    for n in range(7, -1, -1):
        s = s * y + (-1) ** n / math.factorial(2 * n + 1)
        c = c * y + (-1) ** n / math.factorial(2 * n)
    return c, s * x


def powers(c, s):
    table = {1: (c, s)}
    for n in range(2, SG // 2 + 1):
        (ca, sa), (cb, sb) = table[n // 2], table[n - n // 2]
        table[n] = (ca * cb - sa * sb, ca * sb + sa * cb)
    return table


def image_kernel(
    owner, place, model, vis, mix, coords, factor, facets, turned, resid, base, left, right
):
    half = SG // 2

    def clear(index, carry):
        facets[index] = jnp.zeros((FACET, 128), F32)
        return carry

    lax.fori_loop(0, facets.shape[0], clear, 0)
    lane = lax.broadcasted_iota(jnp.int32, (1, 128), 1)
    low = lane < 64

    def residual_block(index, carry):
        interval = lax.div(index, 4)
        start = pl.multiple_of(lax.rem(index, 4) * 128, 128)
        lanes = pl.ds(start, 128)
        rre, rim = vis[interval, 0, :, lanes], vis[interval, 1, :, lanes]
        for d in range(DIRS):
            mre = model[interval, d, 0, :, lanes].astype(F32)
            mim = model[interval, d, 1, :, lanes].astype(F32)
            wre = mix[interval, d : d + 1, lanes]
            wim = mix[interval, d + 16 : d + 17, lanes]
            rre = rre - (wre * mre - wim * mim)
            rim = rim - (wre * mim + wim * mre)
        turned[pl.ds(start, 128), :] = jnp.concatenate([rre, rim], axis=0).T
        return carry

    def group(index, carry):
        interval = lax.div(index, NSUB // GROUP)
        first = pl.multiple_of(lax.rem(index, NSUB // GROUP) * GROUP, GROUP)
        rows = pl.ds(first, GROUP)
        re = jnp.concatenate([resid[0, h, rows, :] for h in range(HALVES)], axis=1)
        im = jnp.concatenate([resid[1, h, rows, :] for h in range(HALVES)], axis=1)

        def angles(which):
            c = jnp.concatenate([base[2 * which, h, rows, :] for h in range(HALVES)], axis=1)
            s = jnp.concatenate([base[2 * which + 1, h, rows, :] for h in range(HALVES)], axis=1)
            return powers(c, s)

        def put(table, part, pixel, value):
            for h in range(HALVES):
                table[h, pl.ds(part * SG + pixel, GROUP, stride=2 * SG), :] = value[
                    :, h * 128 : h * 128 + 128
                ]

        put(left, 0, half, re)
        put(left, 1, half, im)
        for n, (c, s) in angles(0).items():
            rc, rs, ic, js = re * c, re * s, im * c, im * s
            if n < half:
                put(left, 0, half + n, rc - js)
                put(left, 1, half + n, rs + ic)
            put(left, 0, half - n, rc + js)
            put(left, 1, half - n, ic - rs)
        put(right, 0, half, jnp.ones_like(re))
        put(right, 1, half, jnp.zeros_like(re))
        for n, (c, s) in angles(1).items():
            if n < half:
                put(right, 0, half + n, c)
                put(right, 1, half + n, s)
            put(right, 0, half - n, c)
            put(right, 1, half - n, -s)
        sign = jnp.where(low, -1.0, 1.0)
        inside = lax.rem(lane, 64) < SG
        for j in range(GROUP):
            span = slice(j * 2 * SG, (j + 1) * 2 * SG)
            lhs = jnp.concatenate([left[h, span, :] for h in range(HALVES)], axis=1)
            rhs = jnp.concatenate([right[h, span, :] for h in range(HALVES)], axis=1)
            lhs_hi, rhs_hi = lhs.astype(BF16), rhs.astype(BF16)
            lhs_lo = (lhs - lhs_hi.astype(F32)).astype(BF16)
            rhs_lo = (rhs - rhs_hi.astype(F32)).astype(BF16)
            both = lax.dot_general(
                jnp.concatenate([lhs_hi, lhs_lo], axis=0),
                jnp.concatenate([rhs_hi[0:SG], rhs_lo[0:SG], rhs_hi[SG:], rhs_lo[SG:]], axis=0),
                (((1,), (1,)), ((), ())),
                preferred_element_type=F32,
            )
            real = both[0:SG] + both[2 * SG : 3 * SG]
            imag = both[SG : 2 * SG] + both[3 * SG :]
            image = real + sign * pltpu.roll(imag, 64, axis=1)
            image = image + pltpu.roll(image, 128 - SG, axis=1)
            image = jnp.where(inside, image, 0.0)
            at = owner[interval, first + j]
            across = place[interval, 1, first + j]
            down = place[interval, 0, first + j]
            image = pltpu.roll(image, across, axis=1)
            facets[at, pl.ds(down, SG), :] += image
        return carry

    for interval in range(INTERVALS):
        lax.fori_loop(interval * 4, interval * 4 + 4, residual_block, 0)
        scale = 2.0 / (math.sqrt(INTERVALS * NSUB) * math.sqrt(CH * RPS))
        for h in range(HALVES):
            one = turned[pl.ds(2 * h, NSUB, stride=RPS), :] * scale
            two = turned[pl.ds(2 * h + 1, NSUB, stride=RPS), :] * scale
            resid[0, h] = jnp.where(low, one, pltpu.roll(two, 64, axis=1))
            resid[1, h] = jnp.where(low, pltpu.roll(one, 64, axis=1), two)
            for which in range(2):
                at = which * RPS + 2 * h
                coord = jnp.where(
                    low, coords[interval, :, at : at + 1], coords[interval, :, at + 1 : at + 2]
                )
                c, s = sincos(coord * factor[...] * (2.0 * math.pi / SG))
                base[2 * which, h] = c
                base[2 * which + 1, h] = s
        per = NSUB // GROUP
        lax.fori_loop(interval * per, interval * per + per, group, 0)


def local_facets(model, visibilities, mix, uv, owner, place):
    devices = lax.axis_size("freq") * lax.axis_size("bl")
    channel = lax.axis_index("freq") * CH + jnp.arange(CH, dtype=jnp.int32)
    factor = 1.0 + 0.5 * channel.astype(F32) / (lax.axis_size("freq") * CH)
    factor = jnp.concatenate([factor, factor])[None, :]
    coords = uv.reshape(INTERVALS, 2, NSUB, RPS).transpose(0, 2, 1, 3).reshape(INTERVALS, NSUB, 8)
    owner = owner[:, 0, :, 0]
    owner = (owner % 2) * (devices // 2) + owner // 2
    place = place[:, 0].transpose(0, 2, 1)
    vmem = pl.BlockSpec(memory_space=pltpu.VMEM)
    smem = pl.BlockSpec(memory_space=pltpu.SMEM)
    return pl.pallas_call(
        image_kernel,
        out_shape=jax.ShapeDtypeStruct((devices, FACET, 128), F32),
        in_specs=[smem, smem, vmem, vmem, vmem, vmem, vmem],
        out_specs=vmem,
        scratch_shapes=[
            pltpu.VMEM((ROWS, 128), F32),
            pltpu.VMEM((2, HALVES, NSUB, 128), F32),
            pltpu.VMEM((4, HALVES, NSUB, 128), F32),
            pltpu.VMEM((HALVES, GROUP * 2 * SG, 128), F32),
            pltpu.VMEM((HALVES, GROUP * 2 * SG, 128), F32),
        ],
        compiler_params=pltpu.CompilerParams(vmem_limit_bytes=48 * 1024 * 1024),
        name="image",
    )(owner, place, model, visibilities, mix, coords, factor)


PARTS = ((0, 24, (0, 1, 2)), (24, 24, (1, 2, 0)), (48, 16, (2, 0, 1)))


def collect_kernel(facets, out, *scratch):
    sibling, one, two, three, s1, s2, s3 = (scratch[3 * n : 3 * n + 3] for n in range(7))
    core_send, core_recv, send, recv = scratch[21:]
    freq = lax.axis_index("freq")
    bl = lax.axis_index("bl")
    core = lax.rem(bl, 2)
    here = (freq, lax.div(bl, 8), lax.rem(lax.div(bl, 2), 4))

    def device(at, core):
        return (at[0], at[1] * 8 + at[2] * 2 + core)

    def peer(axis, step):
        other = lax.rem(here[axis] + step, 4)
        at = list(here)
        at[axis] = other
        return other, device(at, core)

    barrier = pltpu.get_barrier_semaphore()
    pl.semaphore_signal(barrier, inc=1, device_id=device(here, 1 - core), device_id_type=MESH)
    for axis in range(3):
        for step in range(1, 4):
            pl.semaphore_signal(barrier, inc=1, device_id=peer(axis, step)[1], device_id_type=MESH)
    pl.semaphore_wait(barrier, 10)

    def core_copy(p):
        first, rows, _ = PARTS[p]
        return pltpu.make_async_remote_copy(
            src_ref=facets.at[1 - core, :, :, :, pl.ds(first, rows), :],
            dst_ref=sibling[p],
            send_sem=core_send.at[p],
            recv_sem=core_recv.at[p],
            device_id=device(here, 1 - core),
            device_id_type=MESH,
        )

    def stage_copy(stage, p, step):
        axis = PARTS[p][2][stage]
        other, target = peer(axis, step)
        source, into = ((one, s1), (two, s2), (three, s3))[stage]
        return pltpu.make_async_remote_copy(
            src_ref=source[p].at[other],
            dst_ref=into[p].at[step - 1],
            send_sem=send.at[stage, p, step],
            recv_sem=recv.at[stage, p, step],
            device_id=target,
            device_id_type=MESH,
        )

    for p in range(3):
        core_copy(p).start()
    for p in range(3):
        first, rows, order = PARTS[p]
        core_copy(p).wait_recv()

        def add(index, carry, p=p, first=first, rows=rows, order=order):
            at = (lax.div(index, 16), lax.rem(lax.div(index, 4), 4), lax.rem(index, 4))
            i, j, k = (at[axis] for axis in order)
            one[p][i, j, k] = (
                facets[core, at[0], at[1], at[2], pl.ds(first, rows), :]
                + sibling[p][at[0], at[1], at[2]]
            )
            return carry

        lax.fori_loop(0, 64, add, 0, unroll=4)
        for step in range(1, 4):
            stage_copy(0, p, step).start()
    for stage in range(3):
        source, into = ((one, s1), (two, s2), (three, s3))[stage]
        for p in range(3):
            first, rows, order = PARTS[p]
            mine = here[order[stage]]
            for step in range(1, 4):
                stage_copy(stage, p, step).wait_recv()
            total = source[p][mine] + into[p][0] + into[p][1] + into[p][2]
            if stage < 2:
                (two, three)[stage][p][...] = total
                for step in range(1, 4):
                    stage_copy(stage + 1, p, step).start()
            else:
                out[first : first + rows, :] = total
    for p in range(3):
        core_copy(p).wait_send()
        for stage in range(3):
            for step in range(1, 4):
                stage_copy(stage, p, step).wait_send()


def collect(facets):
    vmem = pl.BlockSpec(memory_space=pltpu.VMEM)
    leads = ((4, 4, 4), (4, 4, 4), (4, 4), (4,), (3, 4, 4), (3, 4), (3,))
    return pl.pallas_call(
        collect_kernel,
        out_shape=jax.ShapeDtypeStruct((FACET, 128), F32),
        in_specs=[vmem],
        out_specs=vmem,
        scratch_shapes=[
            pltpu.VMEM(lead + (rows, 128), F32) for lead in leads for _, rows, _ in PARTS
        ]
        + [
            pltpu.SemaphoreType.DMA((3,)),
            pltpu.SemaphoreType.DMA((3,)),
            pltpu.SemaphoreType.DMA((3, 3, 4)),
            pltpu.SemaphoreType.DMA((3, 3, 4)),
        ],
        compiler_params=pltpu.CompilerParams(
            collective_id=1, has_side_effects=True, vmem_limit_bytes=32 * 1024 * 1024
        ),
        name="collect",
    )(facets.reshape(2, 4, 4, 4, FACET, 128))


def body(visibilities, model, pairs, uv, held_gains, solver_owner, facet_owner, subgrid_pos):
    gains, mix = solve(model, visibilities, pairs, held_gains[0], solver_owner)
    facets = local_facets(model, visibilities, mix, uv, facet_owner, subgrid_pos)
    facet = collect(facets)
    facet = facet.reshape(FACET, 2, FACET).transpose(1, 0, 2)
    return (gains.reshape(INTERVALS, 2, DIRS, STATIONS), facet[None, None])


def solution(mesh):
    placed = (
        P(None, None, "freq", "bl"),
        P(None, None, None, "freq", "bl"),
        P(None, "bl", None),
        P(None, None, "bl"),
        P("bl", None, None, None, None),
        P(),
        P(None, "freq", "bl", None),
        P(None, "freq", "bl", None),
    )
    return jax.shard_map(
        body,
        mesh=mesh,
        in_specs=placed,
        out_specs=(P(), P("freq", "bl", None, None, None)),
        check_vma=False,
    )
```

time: 1610 us -> 173 us (0.11)
  waiting for transfers between devices: 1070 us -> 0 us
  matrix products: 269 us -> 0 us
  other arithmetic: 177 us -> 2.45 us
  Pallas kernels: 0 us -> 163 us
  starting transfers between devices: 33.7 us -> 0 us
  local copies, waits for them, and re-layouts: 36.8 us -> 6.05 us
  between operations: 17.4 us -> 0.72 us
    psum x9 -> x0, waiting for transfers between devices: 1050 us -> none  [the longest x8 1050 us: body(): lax.psum((to_stations(left_re, right_re), to_stations(left_im, right_im),...]
    dot_general x84 -> x0, matrix products: 269 us -> none  [the longest x2 44.6 us: phase_image(): jnp.einsum('jak,jbk->jab', weight_re, vcos, precision=highest)]
    pallas_call x0 -> x3, Pallas kernels: none -> 163 us  [the longest x1 99.6 us: solve(): pl.pallas_call(solve_kernel, out_shape=(jax.ShapeDtypeStruct((INTERVALS,...]
    dot_general x8 -> x0, other arithmetic: 119 us -> none  [the longest x2 29.7 us: phase_image(): jnp.einsum('jak,jbk->jab', weight_im, vsin, precision=highest)]
    reduce_sum x18 -> x0, other arithmetic: 47.4 us -> none  [the longest x9 26 us: predict(): resid_re = vis_re - jnp.sum(first_re * zeta_re - first_im * zeta_im, axis=0)]
    all_to_all x4 -> x0, starting transfers between devices: 32.6 us -> none  [the longest x2 21.3 us: body(): lax.all_to_all(out_pos, ('freq', 'bl'), split_axis=0, concat_axis=0, tile...]
  transfers between devices with their start and end apart: 13 -> 0, of which waited for: 9 -> 0; matrix products, arithmetic and copies ran while one was open for 19% -> 0% of each run, Pallas kernels for 0% -> 0%
where the time goes in v1:
time: 173 us; the launch traced here: 172 us
  Pallas kernels  163 us (94%)
  local copies, waits for them, and re-layouts  6.05 us (3%)
  other arithmetic  2.45 us (1%)
    pallas_call x1, Pallas kernels, solve(): pl.pallas_call(solve_kernel, out_shape=(jax.ShapeDtypeStruct((INTERVALS,...  99.6 us
    pallas_call x1, Pallas kernels, local_facets(): pl.pallas_call(image_kernel, out_shape=jax.ShapeDtypeStruct((devices, FAC...  38.6 us
    pallas_call x1, Pallas kernels, collect(): pl.pallas_call(collect_kernel, out_shape=jax.ShapeDtypeStruct((FACET, 128...  25.1 us

profile of v1, /device:TPU:1, one launch (start us, length us, event | category | flops | bytes accessed | tf_op | source)
XLA Modules:
  0.0 172.4 jit_solution(10502813498237425137)
XLA Ops:
  0.6 0.1 maximum_bitcast_fusion.factor
  0.7 0.7 fusion.2
  1.4 0.7 fusion.1.owner
  2.1 0.7 reshape.26.prow
  2.8 0.1 broadcast_in_dim.27
  2.9 0.0 copy-start.1
  2.9 1.0 broadcast_select_fusion
  3.9 1.0 reshape.28
  4.9 0.1 copy.13
  5.0 0.1 copy.14.coords
  5.1 1.6 reshape_reshape.4.pcol
  6.8 0.0 copy-start
  6.8 1.0 copy-done
  7.8 99.6 %solve.1 = (f32[2,32,512]{2,1,0:T(8,128)S(1)}, f32[2,32,512]{2,1,0:T(8,128)S(1)}) custom-call(bf16[2,16,2,64,512]{4,3,2,1,0:T(8,128)(2,1)} %model.3, f32[2,2,64,512]{3,2,1,0:T(8,128)S(1)} %copy-done, s32[2,1,1024]{2,1,0:T(1,128)S(1)} %reshape.26.prow, s32[2,1024,1]{2,1,0:T(8,128)S(1)} %reshape_reshape.4.pcol, f32[2,48,512]{2,1,0:T(8,128)S(1)} %pad_maximum_fusion.start), custom_call_target="tpu_custom_call" | custom-call | tf_op jit(solution)/shard_map/solve/pallas_call | solution.py:287
  107.4 0.0 copy-done.1
  107.4 38.6 %image.1 = f32[128,64,128]{2,1,0:T(8,128)S(1)} custom-call(s32[2,128]{1,0:T(2,128)S(1)} %fusion.1.owner, s32[2,2,128]{2,1,0:T(2,128)S(1)} %bitcast.19, bf16[2,16,2,64,512]{4,3,2,1,0:T(8,128)(2,1)} %model.3, f32[2,2,64,512]{3,2,1,0:T(8,128)S(1)} %copy-done, f32[2,32,512]{2,1,0:T(8,128)S(1)} %get-tuple-element.5.mix, f32[2,128,8]{2,1,0:T(8,128)S(1)} %copy.14.coords, ...), custom_call_target="tpu_custom_call" | custom-call | tf_op jit(solution)/shard_map/image/pallas_call | solution.py:464
  146.0 25.1 %collect.1 = f32[64,128]{1,0:T(8,128)S(1)} custom-call(f32[2,4,4,4,64,128]{5,4,3,2,1,0:T(8,128)S(1)} %bitcast.17), custom_call_target="tpu_custom_call" | custom-call | tf_op jit(solution)/shard_map/collect/pallas_call | solution.py:574
  171.0 0.1 reshape.31
  171.1 0.6 copy.17
  171.8 0.7 copy.19
  (2 shorter events, 0.0 us)
Async XLA Ops:
  2.9 104.5 %copy-start.1 = (s32[2,1,128,2]{2,3,1,0:T(2,128)S(1)}, s32[2,1,128,2]{2,3,1,0:T(2,128)}, u32[]{:S(2)}) copy-start(s32[2,1,128,2]{2,3,1,0:T(2,128)} %param.15) | copy-start | bytes 6148
  6.8 1.0 copy-start
